TPU v7x, 256 devices: a whole 4x4x8 slice. The times are simulated.
256 devices in a mesh: veh: 32 (over z, x), req: 8 (over y, core).
Axes of the slice: x: 4, y: 4, z: 8, core: 2. Of those that a mesh axis runs over, the one named last changes fastest.
Arguments:
- vehicle_emb: bfloat16 [32768, 128], P(('veh', 'req')), may hold values from -40 to 40
- request_emb: bfloat16 [32768, 128], P('req'), may hold values from -8 to 8
- request_feat: bfloat16 [32768, 256], P('req'), may hold values from -6 to 6
- log_supply: float32 [32768], P('veh'), may hold values from -1.2 to 1.2
- log_demand: float32 [32768], P('req'), may hold values from -1.2 to 1.2
Outputs:
- assigned: float32 [32768, 256], P(('veh', 'req'))
All inputs are finite; a program needn't handle non-finite values.
Results may differ from a plain program's by a relative error of at most 0.0017.
Values may be sent and summed in bfloat16 or wider, within the bound.
A program may use at most 64 MiB of HBM per device.

v0:
```python
import math
import jax
import jax.numpy as jnp
from jax import lax
from jax.sharding import PartitionSpec as P


def local(vehicle_emb, request_emb, request_feat, log_supply, log_demand):
    own_rows = lax.all_gather(vehicle_emb, "req", axis=0, tiled=True)
    row_count = own_rows.shape[0]
    block_rows = min(256, row_count)
    block_count = row_count // block_rows
    vehicle_blocks = own_rows.reshape(block_count, block_rows, own_rows.shape[1])
    score_scale = 3.0 / math.sqrt(own_rows.shape[1])
    request_count = request_emb.shape[0]

    def block_scores(vehicle_block):
        return (
            lax.dot_general(
                vehicle_block,
                request_emb,
                (((1,), (1,)), ((), ())),
                preferred_element_type=jnp.float32,
            )
            * score_scale
        )

    def column_pot(shift):
        shift_blocks = shift.reshape(block_count, block_rows)

        def column_step(state_pair, element):
            running, accrued = state_pair
            vehicle_block, shift_block = element
            logits = block_scores(vehicle_block) + shift_block[:, None]
            highest = jnp.maximum(running, jnp.max(logits, axis=0))
            accrued = accrued * jnp.exp(running - highest) + jnp.sum(
                jnp.exp(logits - highest[None, :]), axis=0
            )
            return ((highest, accrued), None)

        start_pair = (
            jnp.full((request_count,), -1e30, jnp.float32),
            jnp.zeros((request_count,), jnp.float32),
        )
        (highest, accrued), unused = lax.scan(
            column_step, start_pair, (vehicle_blocks, shift_blocks)
        )
        summit = lax.pmax(highest, "veh")
        accrued = lax.psum(accrued * jnp.exp(highest - summit), "veh")
        highest = summit
        return log_demand - (highest + jnp.log(accrued))

    demand_first = column_pot(jnp.zeros((row_count,), jnp.float32))

    def row_block(vehicle_block):
        logits = block_scores(vehicle_block) + demand_first[None, :]
        highest = jnp.max(logits, axis=1)
        return (highest, jnp.sum(jnp.exp(logits - highest[:, None]), axis=1))

    highest, accrued = lax.map(row_block, vehicle_blocks)
    highest = highest.reshape(row_count)
    accrued = accrued.reshape(row_count)
    summit = lax.pmax(highest, "req")
    accrued = lax.psum(accrued * jnp.exp(highest - summit), "req")
    highest = summit
    supply_pot = log_supply - (highest + jnp.log(accrued))
    demand_second = column_pot(supply_pot)

    def assign_block(vehicle_block):
        logits = block_scores(vehicle_block) + demand_second[None, :]
        block_peak = jnp.max(logits, axis=1)
        powers = jnp.exp(logits - block_peak[:, None])
        block_mass = jnp.sum(powers, axis=1)
        weights = powers.astype(jnp.bfloat16)
        block_feat = jnp.dot(weights, request_feat, preferred_element_type=jnp.float32)
        return (block_peak, block_mass, block_feat)

    peaks, masses, features = lax.map(assign_block, vehicle_blocks)
    peaks = peaks.reshape(row_count)
    masses = masses.reshape(row_count)
    features = features.reshape(row_count, request_feat.shape[1])
    summit = lax.pmax(peaks, "req")
    factor = jnp.exp(peaks - summit)
    own_feat, own_mass = (
        lax.psum_scatter(features * factor[:, None], "req", scatter_dimension=0, tiled=True),
        lax.psum_scatter(masses * factor, "req", scatter_dimension=0, tiled=True),
    )
    result = own_feat / own_mass[:, None]
    return result


def solution(mesh):
    in_specs = (P(("veh", "req"), None), P("req", None), P("req", None), P("veh"), P("req"))
    out_specs = P(("veh", "req"), None)
    return jax.shard_map(local, mesh=mesh, in_specs=in_specs, out_specs=out_specs, check_vma=False)
```

profile of v0, /device:TPU:2, one launch (start us, length us, event | category | flops | bytes accessed | tf_op | source)
XLA Modules:
  0.0 732.8 jit_solution(6975081202595240819)
XLA Ops:
  6.5 13.6 %all_gather.3 = bf16[1024,128]{1,0:T(8,128)(2,1)S(1)} all-gather(bf16[128,128]{1,0:T(8,128)(2,1)} %param.13), channel_id=1, replica_groups=mesh['veh'=32,'req'=8] {'req'}, dimensions={0}, use_global_device_ids=true | all-gather | bytes 294912 | tf_op jit(solution)/shard_map/all_gather | solution.py:9
  20.1 26.8 %while.54 = (s32[]{:T(128)}, f32[4096]{0:T(1024)S(1)}, f32[4096]{0:T(1024)S(1)}, bf16[4,256,128]{2,1,0:T(8,128)(2,1)S(1)}, bf16[4096,128]{1,0:T(8,128)(2,1)}, /*index=5*/s32[]{:T(128)}, s32[]{:T(128)}) while((s32[]{:T(128)}, f32[4096]{0:T(1024)S(1)}, f32[4096]{0:T(1024)S(1)}, bf16[4,256,128]{2,1,0:T(8,128)(2,1)S(1)}, ...), condition=%wide.region_3.4_spmd.clone, body=%wide.region_0.3_spmd.clone.sunk | while | flops 272650240 | bytes 9715804 | solution.py:45
  20.1 3.9 fusion.61
  24.0 2.8 exponential_reduce_fusion.7
  26.8 3.9 fusion.61
  30.7 2.8 exponential_reduce_fusion.7
  33.5 3.9 fusion.61
  40.2 3.9 fusion.61
  46.9 140.6 %pmax.28 = f32[4096]{0:T(1024)S(1)} all-reduce(f32[4096]{0:T(1024)S(1)} %get-tuple-element.143), channel_id=1, replica_groups=mesh['veh'=32,'req'=8] {'veh'}, use_global_device_ids=true, to_apply=%region_4.5 | all-reduce | flops 4096 | bytes 32768 | tf_op jit(solution)/shard_map/pmax | solution.py:48
  187.6 139.9 %psum.21 = f32[4096]{0:T(1024)S(1)} all-reduce(f32[4096]{0:T(1024)S(1)} %exponential_multiply_fusion.1), channel_id=1, replica_groups=mesh['veh'=32,'req'=8] {'veh'}, use_global_device_ids=true, to_apply=%region_5.6 | all-reduce | flops 4096 | bytes 32768 | tf_op jit(solution)/shard_map/psum | solution.py:49
  327.6 11.3 %while.52 = (s32[]{:T(128)}, f32[4,256]{1,0:T(4,128)S(1)}, f32[4,256]{1,0:T(4,128)S(1)}, bf16[4,256,128]{2,1,0:T(8,128)(2,1)S(1)}, bf16[4096,128]{1,0:T(8,128)(2...) while((s32[]{:T(128)}, f32[4,256]{1,0:T(4,128)S(1)}, f32[4,256]{1,0:T(4,128)S(1)}, ...), condition=%wide.region_9.10_spmd, body=%wide.region_6.9_spmd.sunk | while | flops 273677824 | bytes 9526369 | solution.py:60
  338.9 12.4 %pmax.29 = f32[1024]{0:T(1024)S(1)} all-reduce(f32[1024]{0:T(1024)S(1)} %bitcast.84), channel_id=1, replica_groups=mesh['veh'=32,'req'=8] {'req'}, use_global_device_ids=true, to_apply=%region_10.11 | all-reduce | flops 1024 | bytes 8192 | tf_op jit(solution)/shard_map/pmax | solution.py:63
  351.4 12.4 %psum.22 = f32[1024]{0:T(1024)S(1)} all-reduce(f32[1024]{0:T(1024)S(1)} %exponential_multiply_fusion.2), channel_id=1, replica_groups=mesh['veh'=32,'req'=8] {'req'}, use_global_device_ids=true, to_apply=%region_11.12 | all-reduce | flops 1024 | bytes 8192 | tf_op jit(solution)/shard_map/psum | solution.py:64
  363.8 27.0 %while.55 = (s32[]{:T(128)}, f32[4096]{0:T(1024)S(1)}, f32[4096]{0:T(1024)S(1)}, bf16[4,256,128]{2,1,0:T(8,128)(2,1)S(1)}, bf16[4096,128]{1,0:T(8,128)(2,1)}, /*index=5*/f32[4,256]{1,0:T(4,128)S(1)}, s32[]{:T(128)}, s32[]{:T(128)}) while((s32[]{:T(128)}, f32[4096]{0:T(1024)S(1)}, f32[4096]{0:T(1024)S(1)}, ...), condition=%wide.region_15.16_spmd.clone, body=%wide.region_12.15_spmd.clone.sunk | while | flops 273698816 | bytes 9718888 | solution.py:45
  363.9 4.0 fusion.64
  370.7 3.9 fusion.64
  377.4 3.9 fusion.64
  384.2 3.9 fusion.64
  390.9 137.7 %pmax.30 = f32[4096]{0:T(1024)S(1)} all-reduce(f32[4096]{0:T(1024)S(1)} %get-tuple-element.147), channel_id=1, replica_groups=mesh['veh'=32,'req'=8] {'veh'}, use_global_device_ids=true, to_apply=%region_16.17 | all-reduce | flops 4096 | bytes 32768 | tf_op jit(solution)/shard_map/pmax | solution.py:48
  528.5 137.7 %psum.23 = f32[4096]{0:T(1024)S(1)} all-reduce(f32[4096]{0:T(1024)S(1)} %exponential_multiply_fusion), channel_id=1, replica_groups=mesh['veh'=32,'req'=8] {'veh'}, use_global_device_ids=true, to_apply=%region_17.18 | all-reduce | flops 4096 | bytes 32768 | tf_op jit(solution)/shard_map/psum | solution.py:49
  666.3 14.6 %while.53 = (s32[]{:T(128)}, f32[4,256]{1,0:T(4,128)S(1)}, f32[4,256]{1,0:T(4,128)S(1)}, f32[4,256,256]{2,1,0:T(8,128)S(1)}, bf16[4,256,128]{2,1,0:T(8,128)(2,1)...) while((s32[]{:T(128)}, f32[4,256]{1,0:T(4,128)S(1)}, ...), condition=%wide.region_21.22_spmd, body=%wide.region_18.21_spmd.sunk | while | flops 812645888 | bytes 16081013 | solution.py:78
  680.9 12.4 %pmax.31 = f32[1024]{0:T(1024)S(1)} all-reduce(f32[1024]{0:T(1024)S(1)} %bitcast.82), channel_id=1, replica_groups=mesh['veh'=32,'req'=8] {'req'}, use_global_device_ids=true, to_apply=%region_22.23 | all-reduce | flops 1024 | bytes 8192 | tf_op jit(solution)/shard_map/pmax | solution.py:82
  695.9 12.4 %all-reduce = f32[1024]{0:T(1024)S(1)} all-reduce(f32[1024]{0:T(1024)S(1)} %get-tuple-element.241), channel_id=3, replica_groups=mesh['veh'=32,'req'=8] {'req'}, use_global_device_ids=true, to_apply=%region_24.25.clone | all-reduce | flops 1024 | bytes 8192
  708.4 16.0 %reduce-scatter.2.cloned.1.call-done = f32[128,256]{1,0:T(8,128)} async-done(((f32[1024,256]{1,0:T(8,128)}), f32[128,256]{1,0:T(8,128)}) %reduce-scatter.2.cloned.1.call-update) | async-done | bytes 131088 | tf_op jit(solution)/shard_map/reduce_scatter | solution.py:85
  (105 shorter events, 46.4 us)
Async XLA Ops:
  6.5 717.8 %reduce-scatter.2.cloned.1.call-start = ((), (), s32[]{:S(2)}) async-start(), calls=%async_computation.1 | async-start | bytes 1179648 | tf_op jit(solution)/shard_map/reduce_scatter | solution.py:85
  20.1 307.4 %copy-start.1 = (f32[4096]{0:T(1024)S(1)}, f32[4096]{0:T(1024)}, u32[]{:S(2)}) copy-start(f32[4096]{0:T(1024)} %param.17) | copy-start | bytes 49156
  327.5 36.2 %copy-start.2 = (f32[1024]{0:T(1024)S(1)}, f32[1024]{0:T(1024)}, u32[]{:S(2)}) copy-start(f32[1024]{0:T(1024)} %param.16) | copy-start | bytes 12292
  363.8 302.4 %copy-start = (bf16[4096,256]{1,0:T(8,128)(2,1)S(1)}, bf16[4096,256]{1,0:T(8,128)(2,1)}, u32[]{:S(2)}) copy-start(bf16[4096,256]{1,0:T(8,128)(2,1)} %param.15) | copy-start | bytes 6291460
  666.3 28.3 %copy-start.3 = (u32[256]{0:T(256)S(1)}, u32[256]{0:T(256)}, u32[]{:S(2)}) copy-start(u32[256]{0:T(256)} %constant.71) | copy-start | bytes 3076
Sparse Core Ops, SparseCore 0:
  694.7 29.5 reduce-scatter.1
where the time goes:
time: 734 us; the launch traced here: 733 us
  blocking collectives  619 us (84%)
  matrix products  50.6 us (7%)
  other arithmetic  31.1 us (4%)
  waiting for transfers between devices  16 us (2%)
  between operations  14.2 us (2%)
    pmax x2, blocking collectives, column_pot(): summit = lax.pmax(highest, 'veh')  278 us
    psum x2, blocking collectives, column_pot(): accrued = lax.psum(accrued * jnp.exp(highest - summit), 'veh')  278 us
    dot_general x16, matrix products, block_scores(): lax.dot_general(vehicle_block, request_emb, (((1,), (1,)), ((), ())), pre...  47.3 us
    reduce_sum x8, other arithmetic, column_step(): jnp.sum(jnp.exp(logits - highest[None, :]), axis=0)  22.3 us
    reduce_scatter x1, waiting for transfers between devices, local(): lax.psum_scatter(features * factor[:, None], 'req', scatter_dimension=0,...  16 us
  transfers between devices with their start and end apart: 1, of which 1 were waited for; matrix products, arithmetic and copies ran while one was open for 0% of the time, Pallas kernels for 0%

commit v1 on v0

--- a/solution.py
+++ b/solution.py
@@ -3,6 +3,11 @@
 import jax.numpy as jnp
 from jax import lax
 from jax.sharding import PartitionSpec as P
+from jax.lax import all_gather
+
+
+def update_the_edges(row_data):
+    return all_gather(row_data, "veh").sum(axis=0)
 
 
 def local(vehicle_emb, request_emb, request_feat, log_supply, log_demand):
@@ -46,7 +51,7 @@
             column_step, start_pair, (vehicle_blocks, shift_blocks)
         )
         summit = lax.pmax(highest, "veh")
-        accrued = lax.psum(accrued * jnp.exp(highest - summit), "veh")
+        accrued = update_the_edges(accrued * jnp.exp(highest - summit))
         highest = summit
         return log_demand - (highest + jnp.log(accrued))
 

time: 734 us -> 561 us (0.76)
  blocking collectives: 619 us -> 442 us
    psum x2 -> x0, blocking collectives: 278 us -> none  [column_pot(): accrued = lax.psum(accrued * jnp.exp(highest - summit), 'veh')]
    all_gather x0 -> x2, blocking collectives: none -> 103 us  [update_the_edges(): return all_gather(row_data, 'veh').sum(axis=0)]
where the time goes in v1:
time: 561 us; the launch traced here: 559 us
  blocking collectives  442 us (79%)
  matrix products  53.4 us (10%)
  other arithmetic  32.4 us (6%)
  waiting for transfers between devices  15.2 us (3%)
  between operations  14.2 us (3%)
    pmax x2, blocking collectives, column_pot(): summit = lax.pmax(highest, 'veh')  275 us
    all_gather x2, blocking collectives, update_the_edges(): return all_gather(row_data, 'veh').sum(axis=0)  103 us
    dot_general x16, matrix products, block_scores(): lax.dot_general(vehicle_block, request_emb, (((1,), (1,)), ((), ())), pre...  47.3 us
    reduce_sum x8, other arithmetic, column_step(): jnp.sum(jnp.exp(logits - highest[None, :]), axis=0)  22.3 us
    reduce_scatter x1, waiting for transfers between devices, local(): lax.psum_scatter(features * factor[:, None], 'req', scatter_dimension=0,...  15.2 us
    all_gather x1, blocking collectives, local(): own_rows = lax.all_gather(vehicle_emb, 'req', axis=0, tiled=True)  13.6 us
    pmax x1, blocking collectives, local(): summit = lax.pmax(highest, 'req')  12.4 us
    psum x1, blocking collectives, local(): accrued = lax.psum(accrued * jnp.exp(highest - summit), 'req')  12.4 us
  transfers between devices with their start and end apart: 1, of which 1 were waited for; matrix products, arithmetic and copies ran while one was open for 0% of the time, Pallas kernels for 0%

profile of v1, /device:TPU:2, one launch (start us, length us, event | category | flops | bytes accessed | tf_op | source)
XLA Modules:
  0.0 559.4 jit_solution(13984790037174441909)
XLA Ops:
  6.5 13.6 %all_gather.15 = bf16[1024,128]{1,0:T(8,128)(2,1)S(1)} all-gather(bf16[128,128]{1,0:T(8,128)(2,1)} %param.13), channel_id=1, replica_groups=mesh['veh'=32,'req'=8] {'req'}, dimensions={0}, use_global_device_ids=true | all-gather | bytes 294912 | tf_op jit(solution)/shard_map/all_gather | solution.py:14
  20.1 26.8 %while.54 = (s32[]{:T(128)}, f32[4096]{0:T(1024)S(1)}, f32[4096]{0:T(1024)S(1)}, bf16[4,256,128]{2,1,0:T(8,128)(2,1)S(1)}, bf16[4096,128]{1,0:T(8,128)(2,1)}, /*index=5*/s32[]{:T(128)}, s32[]{:T(128)}) while((s32[]{:T(128)}, f32[4096]{0:T(1024)S(1)}, f32[4096]{0:T(1024)S(1)}, bf16[4,256,128]{2,1,0:T(8,128)(2,1)S(1)}, ...), condition=%wide.region_3.4_spmd.clone, body=%wide.region_0.3_spmd.clone.sunk | while | flops 272650240 | bytes 9715804 | solution.py:50
  20.1 3.9 fusion.61
  24.0 2.8 exponential_reduce_fusion.7
  26.8 3.9 fusion.61
  30.7 2.8 exponential_reduce_fusion.7
  33.5 3.9 fusion.61
  40.2 3.9 fusion.61
  46.9 140.6 %pmax.28 = f32[4096]{0:T(1024)S(1)} all-reduce(f32[4096]{0:T(1024)S(1)} %get-tuple-element.143), channel_id=1, replica_groups=mesh['veh'=32,'req'=8] {'veh'}, use_global_device_ids=true, to_apply=%region_4.5 | all-reduce | flops 4096 | bytes 32768 | tf_op jit(solution)/shard_map/pmax | solution.py:53
  187.6 51.7 %all-gather = f32[131072]{0:T(1024)S(1)} all-gather(f32[4096]{0:T(1024)S(1)} %exponential_multiply_fusion.1), channel_id=2, replica_groups=mesh['veh'=32,'req'=8] {'veh'}, dimensions={0}, use_global_device_ids=true | all-gather | bytes 540672 | tf_op jit(solution)/shard_map/all_gather | solution.py:10
  239.5 11.4 %while.52 = (s32[]{:T(128)}, f32[4,256]{1,0:T(4,128)S(1)}, f32[4,256]{1,0:T(4,128)S(1)}, bf16[4,256,128]{2,1,0:T(8,128)(2,1)S(1)}, bf16[4096,128]{1,0:T(8,128)(2...) while((s32[]{:T(128)}, f32[4,256]{1,0:T(4,128)S(1)}, f32[4,256]{1,0:T(4,128)S(1)}, ...), condition=%wide.region_9.10_spmd, body=%wide.region_6.9_spmd.sunk | while | flops 273677824 | bytes 9526369 | solution.py:65
  250.9 12.4 %pmax.29 = f32[1024]{0:T(1024)S(1)} all-reduce(f32[1024]{0:T(1024)S(1)} %bitcast.84), channel_id=1, replica_groups=mesh['veh'=32,'req'=8] {'req'}, use_global_device_ids=true, to_apply=%region_10.11 | all-reduce | flops 1024 | bytes 8192 | tf_op jit(solution)/shard_map/pmax | solution.py:68
  263.3 12.4 %psum.7 = f32[1024]{0:T(1024)S(1)} all-reduce(f32[1024]{0:T(1024)S(1)} %exponential_multiply_fusion.2), channel_id=1, replica_groups=mesh['veh'=32,'req'=8] {'req'}, use_global_device_ids=true, to_apply=%region_11.12 | all-reduce | flops 1024 | bytes 8192 | tf_op jit(solution)/shard_map/psum | solution.py:69
  275.8 27.0 %while.55 = (s32[]{:T(128)}, f32[4096]{0:T(1024)S(1)}, f32[4096]{0:T(1024)S(1)}, bf16[4,256,128]{2,1,0:T(8,128)(2,1)S(1)}, bf16[4096,128]{1,0:T(8,128)(2,1)}, /*index=5*/f32[4,256]{1,0:T(4,128)S(1)}, s32[]{:T(128)}, s32[]{:T(128)}) while((s32[]{:T(128)}, f32[4096]{0:T(1024)S(1)}, f32[4096]{0:T(1024)S(1)}, ...), condition=%wide.region_15.16_spmd.clone, body=%wide.region_12.15_spmd.clone.sunk | while | flops 273698816 | bytes 9718888 | solution.py:50
  275.8 4.0 fusion.64
  282.7 3.9 fusion.64
  289.4 3.9 fusion.64
  296.1 3.9 fusion.64
  302.9 134.8 %pmax.30 = f32[4096]{0:T(1024)S(1)} all-reduce(f32[4096]{0:T(1024)S(1)} %get-tuple-element.147), channel_id=1, replica_groups=mesh['veh'=32,'req'=8] {'veh'}, use_global_device_ids=true, to_apply=%region_16.17 | all-reduce | flops 4096 | bytes 32768 | tf_op jit(solution)/shard_map/pmax | solution.py:53
  437.7 51.7 %all-gather.1 = f32[131072]{0:T(1024)S(1)} all-gather(f32[4096]{0:T(1024)S(1)} %exponential_multiply_fusion), channel_id=3, replica_groups=mesh['veh'=32,'req'=8] {'veh'}, dimensions={0}, use_global_device_ids=true | all-gather | bytes 540672 | tf_op jit(solution)/shard_map/all_gather | solution.py:10
  489.6 17.4 %while.53 = (s32[]{:T(128)}, f32[4,256]{1,0:T(4,128)S(1)}, f32[4,256]{1,0:T(4,128)S(1)}, f32[4,256,256]{2,1,0:T(8,128)}, bf16[4,256,128]{2,1,0:T(8,128)(2,1)S(1)...) while((s32[]{:T(128)}, f32[4,256]{1,0:T(4,128)S(1)}, ...), condition=%wide.region_21.22_spmd, body=%wide.region_18.21_spmd.sunk | while | flops 812645888 | bytes 16081521 | solution.py:83
  507.1 12.4 %pmax.31 = f32[1024]{0:T(1024)S(1)} all-reduce(f32[1024]{0:T(1024)S(1)} %bitcast.82), channel_id=1, replica_groups=mesh['veh'=32,'req'=8] {'req'}, use_global_device_ids=true, to_apply=%region_22.23 | all-reduce | flops 1024 | bytes 8192 | tf_op jit(solution)/shard_map/pmax | solution.py:87
  523.2 12.4 %all-reduce = f32[1024]{0:T(1024)S(1)} all-reduce(f32[1024]{0:T(1024)S(1)} %get-tuple-element.241), channel_id=5, replica_groups=mesh['veh'=32,'req'=8] {'req'}, use_global_device_ids=true, to_apply=%region_24.25.clone | all-reduce | flops 1024 | bytes 8192
  535.7 15.2 %reduce-scatter.2.cloned.1.call-done = f32[128,256]{1,0:T(8,128)} async-done(((f32[1024,256]{1,0:T(8,128)}), f32[128,256]{1,0:T(8,128)}) %reduce-scatter.2.cloned.1.call-update) | async-done | bytes 131088 | tf_op jit(solution)/shard_map/reduce_scatter | solution.py:90
  (109 shorter events, 50.8 us)
Async XLA Ops:
  6.5 544.3 %reduce-scatter.2.cloned.1.call-start = ((), (), s32[]{:S(2)}) async-start(), calls=%async_computation.1 | async-start | bytes 1179648 | tf_op jit(solution)/shard_map/reduce_scatter | solution.py:90
  20.1 219.4 %copy-start.1 = (f32[4096]{0:T(1024)S(1)}, f32[4096]{0:T(1024)}, u32[]{:S(2)}) copy-start(f32[4096]{0:T(1024)} %param.17) | copy-start | bytes 49156
  239.5 36.3 %copy-start.2 = (f32[1024]{0:T(1024)S(1)}, f32[1024]{0:T(1024)}, u32[]{:S(2)}) copy-start(f32[1024]{0:T(1024)} %param.16) | copy-start | bytes 12292
  275.8 213.8 %copy-start = (bf16[4096,256]{1,0:T(8,128)(2,1)S(1)}, bf16[4096,256]{1,0:T(8,128)(2,1)}, u32[]{:S(2)}) copy-start(bf16[4096,256]{1,0:T(8,128)(2,1)} %param.15) | copy-start | bytes 6291460
  489.6 32.4 %copy-start.3 = (u32[256]{0:T(256)S(1)}, u32[256]{0:T(256)}, u32[]{:S(2)}) copy-start(u32[256]{0:T(256)} %constant.72) | copy-start | bytes 3076
Sparse Core Ops, SparseCore 0:
  522.1 28.7 reduce-scatter.1
